TPU v7x, 512 devices: a whole 4x4x16 slice. The times are simulated.
512 devices in a mesh: row: 32 (over z, core), col: 16 (over x, y).
Axes of the slice: x: 4, y: 4, z: 16, core: 2. Of those that a mesh axis runs over, the one named last changes fastest.
Arguments:
- rhs: bfloat16 [3, 32, 64, 256], P(None, 'row'), may hold values from -6 to 6
- dinv: bfloat16 [3, 32, 256, 256], P(None, 'row'), as said below
- tiles: bfloat16 [2, 32, 32, 256, 256], P(None, 'row', 'col'), may hold values from -0.046875 to 0.046875
- pattern: int32 [2, 2, 32, 32], P(None, None, 'row', 'col'), may hold values from 0 to 31, as said below
Outputs:
- solution: float32 [3, 32, 64, 256], P(None, 'row')
Inputs may be any that keep to these rules, and one draw needn't show every extreme that they name: pattern[0, l, p, t] = p; pattern[1, l, p, t] = j has (j) modulo the size of col equal to t // 2; positions may repeat, and repeated tiles add. `dinv`: lower triangular with a positive diagonal.
All inputs are finite; a program needn't handle non-finite values.
Results may differ from a plain program's by a relative error of at most 0.0055.
Values may be sent and summed in bfloat16 or wider, within the bound.
A program may use at most 64 MiB of HBM per device.

v0:
```python
import jax
import jax.numpy as jnp
from jax import lax
from jax.sharding import PartitionSpec as P


def broadcast(block, axis, holder):
    block = jnp.where(lax.axis_index(axis) == holder, block, jnp.zeros_like(block))
    return lax.psum(block, axis)


def collect(rounded, mine_col, col_count, repeat):
    pieces = []
    for group in range(repeat):
        pieces.append(broadcast(rounded, "row", mine_col + col_count * group))
    return jnp.concatenate(pieces, 0)


def per_device(rhs, dinv, tiles, pattern):
    blocks = rhs.shape[1]
    levels_all = rhs.shape[0]
    col_count = lax.axis_size("col")
    row_count = lax.axis_size("row")
    repeat = row_count // col_count
    mine_row = lax.axis_index("row")
    mine_col = lax.axis_index("col")
    targets = pattern[0, :, 0, :] % blocks
    raw_cols = pattern[1, :, 0, :]
    sources = raw_cols // blocks // col_count * blocks + raw_cols % blocks
    row_pick = (targets[:, None, :] == jnp.arange(blocks, dtype=jnp.int32)[None, :, None]).astype(
        jnp.float32
    )
    col_pick = (
        sources[:, None, :] == jnp.arange(repeat * blocks, dtype=jnp.int32)[None, :, None]
    ).astype(jnp.float32)
    fronts = [rhs]
    forward_all = [[] for front in fronts]
    rounded_all = [None for front in fronts]
    for level_now in range(levels_all):
        front_index = 0
        front_level = fronts[front_index][level_now]
        current = front_level.astype(jnp.float32)
        if level_now > 0:
            nearby = collect(rounded_all[front_index], mine_col, col_count, repeat)
            source = jnp.take(nearby, sources[level_now - 1], axis=0)
            product = jnp.einsum(
                "sjb,sab->sja", source, tiles[level_now - 1, 0], preferred_element_type=jnp.float32
            )
            partial_value = jnp.sum(
                row_pick[level_now - 1][:, :, None, None] * product[None], axis=1
            )
            total_sum = lax.psum(partial_value, "col")
            current = current - total_sum
        solved = jnp.einsum(
            "rjb,rab->rja",
            current.astype(jnp.bfloat16),
            dinv[level_now],
            preferred_element_type=jnp.float32,
        )
        forward_all[front_index].append(solved)
        rounded_all[front_index] = solved.astype(jnp.bfloat16)
    backward_all = [[None] * levels_all for front in fronts]
    following_all = [None for front in fronts]
    for level_now in range(levels_all - 1, -1, -1):
        front_index = 0
        remainder = forward_all[front_index][level_now]
        if level_now < levels_all - 1:
            source = jnp.take(following_all[front_index], targets[level_now], axis=0)
            product = jnp.einsum(
                "sja,sab->sjb", source, tiles[level_now, 0], preferred_element_type=jnp.float32
            )
            partial_value = jnp.sum(col_pick[level_now][:, :, None, None] * product[None], axis=1)
            column_total = lax.psum(partial_value, "row")
            shaped = column_total.reshape((repeat, blocks) + column_total.shape[1:])
            picked = lax.dynamic_index_in_dim(shaped, mine_row // col_count, 0, keepdims=False)
            arrived = broadcast(picked, "col", mine_row % col_count)
            remainder = remainder - arrived
        solved = jnp.einsum(
            "rjb,rba->rja",
            remainder.astype(jnp.bfloat16),
            dinv[level_now],
            preferred_element_type=jnp.float32,
        )
        backward_all[front_index][level_now] = solved
        following_all[front_index] = solved.astype(jnp.bfloat16)
    front_index = 0
    levels_stack = jnp.stack(backward_all[front_index])
    return levels_stack


def solution(mesh):
    in_specs = (
        P(None, "row", None, None),
        P(None, "row", None, None),
        P(None, "row", "col", None, None),
        P(None, None, "row", "col"),
    )
    out_specs = P(None, "row", None, None)
    return jax.shard_map(
        per_device, mesh=mesh, in_specs=in_specs, out_specs=out_specs, check_vma=False
    )
```

profile of v0, /device:TPU:2, one launch (start us, length us, event | category | flops | bytes accessed | tf_op | source)
XLA Modules:
  0.0 1224.9 jit_solution(12864337464634439809)
XLA Ops:
  6.5 1.1 fusion.18
  7.7 0.7 select_bitcast_fusion.3
  8.4 0.0 all-reduce.11.cloned.1.call-start
  8.4 0.7 slice.51
  9.2 188.0 %all-reduce.25.cloned.1.call-done = (bf16[1,64,256]{2,1,0:T(8,128)(2,1)}, bf16[1,64,256]{2,1,0:T(8,128)(2,1)}) async-done(((bf16[1,64,256]{2,1,0:T(8,128)(2,1)}, bf16[1,64,256]{2,1,0:T(8,128)(2,1)}), (bf16[1,64,256]{2,1,0:T(8,128)(2,1)}, bf16[1,64,256]{2,1,0:T(8,128)(2,1)})) %all-reduce.25.cloned.1.call-update) | async-done | bytes 65552 | tf_op jit(solution)/shard_map/psum | solution.py:9
  197.2 0.8 pad_maximum_fusion.1
  198.0 0.5 gather_fusion
  198.6 0.8 convolution_bitcast_fusion.2
  199.5 106.2 %all-reduce.11.cloned.1.call-done = f32[1,64,256]{2,1,0:T(8,128)} async-done(((f32[1,64,256]{2,1,0:T(8,128)}), f32[1,64,256]{2,1,0:T(8,128)}) %all-reduce.11.cloned.1.call-update) | async-done | bytes 65552 | tf_op jit(solution)/shard_map/psum | solution.py:52
  305.7 1.0 fusion.15
  306.7 0.7 select_bitcast_fusion.1
  307.4 183.7 %all-reduce.23.cloned.1.call-done = (bf16[1,64,256]{2,1,0:T(8,128)(2,1)}, bf16[1,64,256]{2,1,0:T(8,128)(2,1)}) async-done(((bf16[1,64,256]{2,1,0:T(8,128)(2,1)}, bf16[1,64,256]{2,1,0:T(8,128)(2,1)}), (bf16[1,64,256]{2,1,0:T(8,128)(2,1)}, bf16[1,64,256]{2,1,0:T(8,128)(2,1)})) %all-reduce.23.cloned.1.call-update) | async-done | bytes 65552 | tf_op jit(solution)/shard_map/psum | solution.py:9
  491.1 0.8 pad_maximum_fusion.2
  491.9 0.5 gather_fusion.1
  492.5 0.8 convolution_bitcast_fusion.1
  493.4 106.0 %all-reduce.13.cloned.1.call-done = f32[1,64,256]{2,1,0:T(8,128)} async-done(((f32[1,64,256]{2,1,0:T(8,128)}), f32[1,64,256]{2,1,0:T(8,128)}) %all-reduce.13.cloned.1.call-update) | async-done | bytes 65552 | tf_op jit(solution)/shard_map/psum | solution.py:52
  599.4 1.1 fusion.57
  600.6 0.2 fusion.1
  600.8 0.7 multiply_reduce_fusion.1
  601.5 0.0 all-reduce.17.cloned.1.call-start
  601.6 195.6 %all-reduce.15.cloned.1.call-done = f32[2,64,256]{2,1,0:T(8,128)} async-done(((f32[2,64,256]{2,1,0:T(8,128)}), f32[2,64,256]{2,1,0:T(8,128)}) %all-reduce.15.cloned.1.call-update) | async-done | bytes 131088 | tf_op jit(solution)/shard_map/psum | solution.py:73
  797.2 1.5 dynamic-slice_select_fusion.1
  798.7 0.0 all-reduce.19.cloned.1.call-start
  798.7 109.0 %all-reduce.17.cloned.1.call-done = f32[1,64,256]{2,1,0:T(8,128)} async-done(((f32[1,64,256]{2,1,0:T(8,128)}), f32[1,64,256]{2,1,0:T(8,128)}) %all-reduce.17.cloned.1.call-update) | async-done | bytes 65552 | tf_op jit(solution)/shard_map/psum | solution.py:9
  907.8 1.0 fusion.62
  908.8 0.2 fusion.4
  908.9 0.8 multiply_reduce_fusion
  909.8 195.9 %all-reduce.19.cloned.1.call-done = f32[2,64,256]{2,1,0:T(8,128)} async-done(((f32[2,64,256]{2,1,0:T(8,128)}), f32[2,64,256]{2,1,0:T(8,128)}) %all-reduce.19.cloned.1.call-update) | async-done | bytes 131088 | tf_op jit(solution)/shard_map/psum | solution.py:73
  1105.7 1.5 dynamic-slice_select_fusion
  1107.2 109.2 %all-reduce.21.cloned.1.call-done = f32[1,64,256]{2,1,0:T(8,128)} async-done(((f32[1,64,256]{2,1,0:T(8,128)}), f32[1,64,256]{2,1,0:T(8,128)}) %all-reduce.21.cloned.1.call-update) | async-done | bytes 65552 | tf_op jit(solution)/shard_map/psum | solution.py:9
  1216.4 1.0 convolution_bitcast_fusion
  1217.4 0.7 pad_maximum_fusion
  (25 shorter events, 0.4 us)
Async XLA Ops:
  6.5 192.0 %copy-start.1 = (bf16[2,1,2,256,256]{4,3,2,1,0:T(8,128)(2,1)S(1)}, bf16[2,1,2,256,256]{4,3,2,1,0:T(8,128)(2,1)}, u32[]{:S(2)}) copy-start(bf16[2,1,2,256,256]{4,3,2,1,0:T(8,128)(2,1)} %param.10) | copy-start | bytes 1572868
  6.5 190.7 %all-reduce.25.cloned.1.call-start = ((), (), s32[]{:S(2)}) async-start(), calls=%async_computation.7 | async-start | bytes 131072 | tf_op jit(solution)/shard_map/psum | solution.py:9
  8.4 297.3 %copy-start = (bf16[3,1,256,256]{3,2,1,0:T(8,128)(2,1)S(1)}, bf16[3,1,256,256]{3,2,1,0:T(8,128)(2,1)}, u32[]{:S(2)}) copy-start(bf16[3,1,256,256]{3,2,1,0:T(8,128)(2,1)} %param.9) | copy-start | bytes 1179652
  8.4 297.3 %all-reduce.11.cloned.1.call-start = ((), (), s32[]{:S(2)}) async-start(), calls=%async_computation | async-start | bytes 131072 | tf_op jit(solution)/shard_map/psum | solution.py:52
  198.6 107.1 %copy-start.2 = (bf16[3,1,64,256]{3,2,1,0:T(8,128)(2,1)S(1)}, bf16[3,1,64,256]{3,2,1,0:T(8,128)(2,1)}, u32[]{:S(2)}) copy-start(bf16[3,1,64,256]{3,2,1,0:T(8,128)(2,1)} %param.8) | copy-start | bytes 294916
  199.4 291.7 %all-reduce.23.cloned.1.call-start = ((), (), s32[]{:S(2)}) async-start(), calls=%async_computation.6 | async-start | bytes 131072 | tf_op jit(solution)/shard_map/psum | solution.py:9
  307.4 292.1 %all-reduce.13.cloned.1.call-start = ((), (), s32[]{:S(2)}) async-start(), calls=%async_computation.1 | async-start | bytes 131072 | tf_op jit(solution)/shard_map/psum | solution.py:52
  493.4 303.8 %all-reduce.15.cloned.1.call-start = ((), (), s32[]{:S(2)}) async-start(), calls=%async_computation.2 | async-start | bytes 262144 | tf_op jit(solution)/shard_map/psum | solution.py:73
  601.5 306.3 %all-reduce.17.cloned.1.call-start = ((), (), s32[]{:S(2)}) async-start(), calls=%async_computation.3 | async-start | bytes 131072 | tf_op jit(solution)/shard_map/psum | solution.py:9
  798.7 307.0 %all-reduce.19.cloned.1.call-start = ((), (), s32[]{:S(2)}) async-start(), calls=%async_computation.4 | async-start | bytes 262144 | tf_op jit(solution)/shard_map/psum | solution.py:73
  909.7 306.7 %all-reduce.21.cloned.1.call-start = ((), (), s32[]{:S(2)}) async-start(), calls=%async_computation.5 | async-start | bytes 131072 | tf_op jit(solution)/shard_map/psum | solution.py:9
Sparse Core Ops, SparseCore 0:
  9.8 187.3 all-reduce.24
  200.7 104.9 all-reduce.10
  308.1 182.9 all-reduce.22
  494.5 104.8 all-reduce.12
  601.7 195.4 all-reduce.14
  800.6 107.1 all-reduce.16
  910.1 195.4 all-reduce.18
  1109.2 107.1 all-reduce.20
where the time goes:
time: 1230 us; the launch traced here: 1220 us
  waiting for transfers between devices  1190 us (97%)
  between operations  13.6 us (1%)
    psum x4, waiting for transfers between devices, broadcast(): return lax.psum(block, axis)  590 us
    psum x2, waiting for transfers between devices, per_device(): column_total = lax.psum(partial_value, 'row')  391 us
    psum x2, waiting for transfers between devices, per_device(): total_sum = lax.psum(partial_value, 'col')  212 us
  transfers between devices with their start and end apart: 8, of which 8 were waited for; matrix products, arithmetic and copies ran while one was open for 0% of the time, Pallas kernels for 0%

commit v1 on v0

--- a/solution.py
+++ b/solution.py
@@ -49,7 +49,13 @@
             partial_value = jnp.sum(
                 row_pick[level_now - 1][:, :, None, None] * product[None], axis=1
             )
-            total_sum = lax.psum(partial_value, "col")
+
+            def samples_handle(x_part):
+                piece_now = lax.all_gather(x_part, axis_name="col")
+                x_new = jnp.sum(piece_now, axis=0)
+                return x_new
+
+            total_sum = samples_handle(partial_value)
             current = current - total_sum
         solved = jnp.einsum(
             "rjb,rab->rja",

time: 1230 us -> 1120 us (0.911)
  waiting for transfers between devices: 1190 us -> 1090 us
    psum x2 -> x0, waiting for transfers between devices: 212 us -> none  [per_device(): total_sum = lax.psum(partial_value, 'col')]
    all_gather x0 -> x2, waiting for transfers between devices: none -> 104 us  [samples_handle(): piece_now = lax.all_gather(x_part, axis_name='col')]
where the time goes in v1:
time: 1120 us
  waiting for transfers between devices  1090 us (97%)
  between operations  13.6 us (1%)
    psum x4, waiting for transfers between devices, broadcast(): return lax.psum(block, axis)  590 us
    psum x2, waiting for transfers between devices, per_device(): column_total = lax.psum(partial_value, 'row')  391 us
    all_gather x2, waiting for transfers between devices, samples_handle(): piece_now = lax.all_gather(x_part, axis_name='col')  104 us
  transfers between devices with their start and end apart: 8, of which 8 were waited for; matrix products, arithmetic and copies ran while one was open for 0% of the time, Pallas kernels for 0%

profile of v1, /device:TPU:2, one launch (start us, length us, event | category | flops | bytes accessed | tf_op | source)
XLA Modules:
  0.0 1117.3 jit_solution(395398026023259927)
XLA Ops:
  6.5 1.1 fusion.18
  7.7 0.7 select_bitcast_fusion.3
  8.4 0.7 slice.51
  9.1 188.1 %all-reduce.19.cloned.1.call-done = (bf16[1,64,256]{2,1,0:T(8,128)(2,1)}, bf16[1,64,256]{2,1,0:T(8,128)(2,1)}) async-done(((bf16[1,64,256]{2,1,0:T(8,128)(2,1)}, bf16[1,64,256]{2,1,0:T(8,128)(2,1)}), (bf16[1,64,256]{2,1,0:T(8,128)(2,1)}, bf16[1,64,256]{2,1,0:T(8,128)(2,1)})) %all-reduce.19.cloned.1.call-update) | async-done | bytes 65552 | tf_op jit(solution)/shard_map/psum | solution.py:9
  197.2 0.8 pad_maximum_fusion.1
  198.0 0.5 gather_fusion
  198.6 0.8 convolution_bitcast_fusion.2
  199.4 0.0 all-reduce.17.cloned.1.call-start
  199.5 52.4 %all-gather.5.cloned.1.call-done = f32[1024,256]{1,0:T(8,128)} async-done(((f32[64,256]{1,0:T(8,128)}), f32[1024,256]{1,0:T(8,128)}) %all-gather.5.cloned.1.call-update) | async-done | bytes 1048592 | tf_op jit(solution)/shard_map/all_gather | solution.py:54
  251.8 1.3 reduce.6
  253.2 0.2 fusion.15
  253.3 0.7 select_bitcast_fusion.1
  254.1 183.3 %all-reduce.17.cloned.1.call-done = (bf16[1,64,256]{2,1,0:T(8,128)(2,1)}, bf16[1,64,256]{2,1,0:T(8,128)(2,1)}) async-done(((bf16[1,64,256]{2,1,0:T(8,128)(2,1)}, bf16[1,64,256]{2,1,0:T(8,128)(2,1)}), (bf16[1,64,256]{2,1,0:T(8,128)(2,1)}, bf16[1,64,256]{2,1,0:T(8,128)(2,1)})) %all-reduce.17.cloned.1.call-update) | async-done | bytes 65552 | tf_op jit(solution)/shard_map/psum | solution.py:9
  437.4 0.8 pad_maximum_fusion.2
  438.2 0.5 gather_fusion.1
  438.7 0.8 convolution_bitcast_fusion.1
  439.7 51.8 %all-gather.7.cloned.1.call-done = f32[1024,256]{1,0:T(8,128)} async-done(((f32[64,256]{1,0:T(8,128)}), f32[1024,256]{1,0:T(8,128)}) %all-gather.7.cloned.1.call-update) | async-done | bytes 1048592 | tf_op jit(solution)/shard_map/all_gather | solution.py:54
  491.4 1.3 reduce.7
  492.7 0.3 fusion.54
  493.0 0.2 fusion.1
  493.2 0.8 multiply_reduce_fusion.1
  494.1 195.6 %all-reduce.9.cloned.1.call-done = f32[2,64,256]{2,1,0:T(8,128)} async-done(((f32[2,64,256]{2,1,0:T(8,128)}), f32[2,64,256]{2,1,0:T(8,128)}) %all-reduce.9.cloned.1.call-update) | async-done | bytes 131088 | tf_op jit(solution)/shard_map/psum | solution.py:79
  689.6 1.5 dynamic-slice_select_fusion.1
  691.2 109.0 %all-reduce.11.cloned.1.call-done = f32[1,64,256]{2,1,0:T(8,128)} async-done(((f32[1,64,256]{2,1,0:T(8,128)}), f32[1,64,256]{2,1,0:T(8,128)}) %all-reduce.11.cloned.1.call-update) | async-done | bytes 65552 | tf_op jit(solution)/shard_map/psum | solution.py:9
  800.2 1.0 fusion.59
  801.2 0.2 fusion.4
  801.4 0.8 multiply_reduce_fusion
  802.2 195.9 %all-reduce.13.cloned.1.call-done = f32[2,64,256]{2,1,0:T(8,128)} async-done(((f32[2,64,256]{2,1,0:T(8,128)}), f32[2,64,256]{2,1,0:T(8,128)}) %all-reduce.13.cloned.1.call-update) | async-done | bytes 131088 | tf_op jit(solution)/shard_map/psum | solution.py:79
  998.1 1.5 dynamic-slice_select_fusion
  999.6 109.2 %all-reduce.15.cloned.1.call-done = f32[1,64,256]{2,1,0:T(8,128)} async-done(((f32[1,64,256]{2,1,0:T(8,128)}), f32[1,64,256]{2,1,0:T(8,128)}) %all-reduce.15.cloned.1.call-update) | async-done | bytes 65552 | tf_op jit(solution)/shard_map/psum | solution.py:9
  1108.8 1.0 convolution_bitcast_fusion
  1109.8 0.7 pad_maximum_fusion
  (27 shorter events, 0.4 us)
Async XLA Ops:
  6.5 192.0 %copy-start.1 = (bf16[2,1,2,256,256]{4,3,2,1,0:T(8,128)(2,1)S(1)}, bf16[2,1,2,256,256]{4,3,2,1,0:T(8,128)(2,1)}, u32[]{:S(2)}) copy-start(bf16[2,1,2,256,256]{4,3,2,1,0:T(8,128)(2,1)} %param.10) | copy-start | bytes 1572868
  6.5 190.7 %all-reduce.19.cloned.1.call-start = ((), (), s32[]{:S(2)}) async-start(), calls=%async_computation.7 | async-start | bytes 131072 | tf_op jit(solution)/shard_map/psum | solution.py:9
  8.4 243.5 %all-gather.5.cloned.1.call-start = ((), (), s32[]{:S(2)}) async-start(), calls=%async_computation.4 | async-start | bytes 1114112 | tf_op jit(solution)/shard_map/all_gather | solution.py:54
  199.4 238.0 %all-reduce.17.cloned.1.call-start = ((), (), s32[]{:S(2)}) async-start(), calls=%async_computation.6 | async-start | bytes 131072 | tf_op jit(solution)/shard_map/psum | solution.py:9
  251.8 1.4 copy-start
  251.8 1.4 copy-start.2
  254.0 237.4 %all-gather.7.cloned.1.call-start = ((), (), s32[]{:S(2)}) async-start(), calls=%async_computation.5 | async-start | bytes 1114112 | tf_op jit(solution)/shard_map/all_gather | solution.py:54
  439.6 250.0 %all-reduce.9.cloned.1.call-start = ((), (), s32[]{:S(2)}) async-start(), calls=%async_computation | async-start | bytes 262144 | tf_op jit(solution)/shard_map/psum | solution.py:79
  494.0 306.2 %all-reduce.11.cloned.1.call-start = ((), (), s32[]{:S(2)}) async-start(), calls=%async_computation.1 | async-start | bytes 131072 | tf_op jit(solution)/shard_map/psum | solution.py:9
  691.1 307.0 %all-reduce.13.cloned.1.call-start = ((), (), s32[]{:S(2)}) async-start(), calls=%async_computation.2 | async-start | bytes 262144 | tf_op jit(solution)/shard_map/psum | solution.py:79
  802.2 306.7 %all-reduce.15.cloned.1.call-start = ((), (), s32[]{:S(2)}) async-start(), calls=%async_computation.3 | async-start | bytes 131072 | tf_op jit(solution)/shard_map/psum | solution.py:9
Sparse Core Ops, SparseCore 0:
  9.8 187.3 all-reduce.18
  200.7 51.1 all-gather.4
  254.4 182.9 all-reduce.16
  440.3 51.1 all-gather.6
  494.1 195.4 all-reduce.8
  693.0 107.1 all-reduce.10
  802.5 195.4 all-reduce.12
  1001.6 107.1 all-reduce.14
